TPU v7x, 512 devices: a whole 4x4x16 slice. The times are simulated.
512 devices in a mesh: pair: 16 (over z_lo, core), aux: 32 (over y, z_hi, x).
Axes of the slice: x: 4, y: 4, z: 16 (z_hi: 2, z_lo: 8; z = z_hi * 8 + z_lo), core: 2. Of those that a mesh axis runs over, the one named last changes fastest.
Arguments:
- integral_strips: bfloat16 [32, 512, 20480], P('pair', None, 'aux'), may hold values from -6 to 6
- slot_row_block: int32 [32], replicated, may hold values from 0 to 47
- slot_strip_index: int32 [32], replicated, may hold values from 0 to 31
- slot_column_block: int32 [32], replicated, may hold values from 0 to 47
- block_live: int32 [32], replicated, may hold values from 0 to 1, as said below
- ao_factor: bfloat16 [6144, 4096], P('pair', 'aux'), may hold values from -6 to 6
- aux_factor: bfloat16 [4096, 20480], P('pair', 'aux'), may hold values from -0.00390625 to 0.00390625
Outputs:
- contraction: float32 [6144, 4096], P('pair', 'aux')
Inputs may be any that keep to these rules, and one draw needn't show every extreme that they name: `block_live`: 1 marks a slot that survives screening; slots k of one index i of the pair axis are i * 2 to (i + 1) * 2 - 1; every index has 1 to 2 live slots, and some index has all 2 live.
All inputs are finite; a program needn't handle non-finite values.
Results may differ from a plain program's by a relative error of at most 0.0003.
Values may be sent and summed in bfloat16 or wider, within the bound.
A program may use at most 64 MiB of HBM per device.

v0:
```python
import jax
import jax.numpy as jnp
from jax import lax
from jax.sharding import PartitionSpec as P

BLOCK_FUNCTIONS = 128


def per_device(
    integral_strips,
    slot_row_block,
    slot_strip_index,
    slot_column_block,
    block_live,
    ao_factor,
    aux_factor,
):
    slot_count = integral_strips.shape[0]
    block_width = BLOCK_FUNCTIONS
    strip_rows = integral_strips.shape[1] // block_width
    strips_block = block_width // strip_rows
    pair_count = lax.axis_size("pair")
    pair_index = lax.axis_index("pair")
    aux_index = lax.axis_index("aux")
    blocks_dev = ao_factor.shape[0] // block_width
    strips_dev = blocks_dev * strips_block
    rank_part = ao_factor.shape[1]
    first_slot = pair_index * slot_count
    rows_mine = lax.dynamic_slice_in_dim(slot_row_block, first_slot, slot_count)
    live_mine = lax.dynamic_slice_in_dim(block_live, first_slot, slot_count).astype(jnp.float32)
    slab_view = ao_factor.reshape(blocks_dev, block_width, rank_part)
    wanted = slot_column_block.reshape(pair_count, slot_count)
    local_index = wanted - pair_index * blocks_dev
    held_here = (local_index >= 0) & (local_index < blocks_dev)
    picked = slab_view[jnp.clip(local_index, 0, blocks_dev - 1)]
    picked = jnp.where(held_here[:, :, None, None], picked, jnp.zeros_like(picked))
    arrived = lax.all_to_all(picked, "pair", split_axis=0, concat_axis=0, tiled=True)
    fetched = jnp.sum(arrived.astype(jnp.float32), axis=0).astype(jnp.bfloat16)
    full_rows = lax.all_gather(fetched, "aux", axis=2, tiled=True)
    segment = lax.all_gather(aux_factor, "pair", axis=0, tiled=True)
    rank_count = segment.shape[0]

    def per_slot(items):
        integrals, rows_here, alive_flag = items
        products = lax.dot_general(
            integrals, segment, (((1,), (1,)), ((), ())), preferred_element_type=jnp.float32
        )
        products = products.reshape(strip_rows, block_width, rank_count)
        return jnp.sum(products * rows_here.astype(jnp.float32)[None], axis=1) * alive_flag

    partial_value = lax.map(per_slot, (integral_strips, full_rows, live_mine))
    summed = lax.psum(partial_value, "aux")
    shared = lax.dynamic_slice_in_dim(summed, aux_index * rank_part, rank_part, 2)
    owner_index = rows_mine // blocks_dev
    routing = (owner_index[None, :] == jnp.arange(pair_count, dtype=jnp.int32)[:, None]).astype(
        jnp.float32
    )
    outgoing = routing[:, :, None, None] * shared[None]
    incoming = lax.all_to_all(outgoing, "pair", split_axis=0, concat_axis=0, tiled=True)
    sources = (slot_row_block - pair_index * blocks_dev) * strips_block + slot_strip_index
    placing = (sources[:, None] == jnp.arange(strips_dev, dtype=jnp.int32)[None, :]).astype(
        jnp.float32
    )
    result = jnp.dot(
        placing.T,
        incoming.reshape(pair_count * slot_count, strip_rows * rank_part),
        precision=lax.Precision.HIGHEST,
    )
    return result.reshape(strips_dev * strip_rows, rank_part)


def solution(mesh):
    in_specs = (P("pair", None, "aux"), P(), P(), P(), P(), P("pair", "aux"), P("pair", "aux"))
    out_specs = P("pair", "aux")
    return jax.shard_map(
        per_device, mesh=mesh, in_specs=in_specs, out_specs=out_specs, check_vma=False
    )
```

profile of v0, /device:TPU:1, one launch (start us, length us, event | category | flops | bytes accessed | tf_op | source)
XLA Modules:
  0.0 913.4 jit_solution(17095800663345495365)
XLA Ops:
  6.6 0.8 subtract_clamp_fusion
  7.4 0.7 compare_and_fusion
  8.3 0.8 gather_fusion
  9.2 63.6 %all_to_all.10 = bf16[16,2,128,128]{3,2,1,0:T(8,128)(2,1)S(1)} all-to-all(bf16[16,2,128,128]{3,2,1,0:T(8,128)(2,1)S(1)} %broadcast_select_fusion), channel_id=1, replica_groups=mesh['pair'=16,'aux'=32] {'pair'}, dimensions={0} | all-to-all | bytes 2097152 | tf_op jit(solution)/shard_map/all_to_all | solution.py:37
  72.9 0.8 reduce_sum.21
  73.7 0.7 all-gather.3.cloned.1.call-update
  74.7 139.8 %all-gather.5.cloned.1.call-done = bf16[2,128,4096]{2,1,0:T(8,128)(2,1)} async-done(((bf16[2,128,128]{2,1,0:T(8,128)(2,1)}), bf16[2,128,4096]{2,1,0:T(8,128)(2,1)}) %all-gather.5.cloned.1.call-update) | async-done | bytes 2097168 | tf_op jit(solution)/shard_map/all_gather | solution.py:39
  214.5 103.8 %all-gather.3.cloned.1.call-done = bf16[4096,640]{1,0:T(8,128)(2,1)} async-done(((bf16[256,640]{1,0:T(8,128)(2,1)}), bf16[4096,640]{1,0:T(8,128)(2,1)}) %all-gather.3.cloned.1.call-update) | async-done | bytes 5242896 | tf_op jit(solution)/shard_map/all_gather | solution.py:40
  318.3 18.3 %while.10 = (s32[]{:T(128)}, f32[2,4,4096]{2,1,0:T(4,128)S(1)}, bf16[2,512,640]{2,1,0:T(8,128)(2,1)S(1)}, bf16[4096,640]{1,0:T(8,128)(2,1)}, bf16[2,128,4096]{2,1,0:T(8,128)(2,1)}, /*index=5*/f32[2]{0:T(128)S(1)}, s32[]{:T(128)}) while((s32[]{:T(128)}, f32[2,4,4096]{2,1,0:T(4,128)S(1)}, bf16[2,512,640]{2,1,0:T(8,128)(2,1)S(1)}, ...), condition=%wide.region_3.4_spmd, body=%wide.region_1.3_spmd.sunk | while | flops 2689073152 | bytes 12648553 | solution.py:51
  318.3 1.4 bitcast_convert_fusion.2
  319.8 6.3 multiply_reduce_fusion.2
  326.2 0.6 dynamic_slice.34
  326.7 0.7 bitcast_dynamic-update-slice_fusion.2
  327.4 1.4 bitcast_convert_fusion.2
  328.9 6.3 multiply_reduce_fusion.2
  335.3 0.6 dynamic_slice.34
  335.9 0.7 bitcast_dynamic-update-slice_fusion.2
  336.6 0.6 copy-done.2
  337.3 531.9 %all-reduce.2.cloned.1.call-done = f32[2,4,4096]{2,1,0:T(4,128)} async-done(((f32[2,4,4096]{2,1,0:T(4,128)}), f32[2,4,4096]{2,1,0:T(4,128)}) %all-reduce.2.cloned.1.call-update) | async-done | bytes 131088 | tf_op jit(solution)/shard_map/psum | solution.py:52
  869.1 0.7 constant_dynamic-slice_fusion.1
  869.8 0.7 broadcast_multiply_fusion
  870.5 25.2 %all-to-all-start.1 = ((f32[16,2,4,128]{3,2,1,0:T(4,128)}), f32[16,2,4,128]{3,2,1,0:T(4,128)S(1)}, u32[]{:S(2)}, u32[]{:S(2)}) async-start(f32[16,2,4,128]{3,2,1,0:T(4,128)} %broadcast_multiply_fusion), calls=%async_computation.1 | async-start | bytes 131072 | tf_op jit(solution)/shard_map/all_to_all | solution.py:59
  895.8 10.1 %all-to-all-done.1 = f32[16,2,4,128]{3,2,1,0:T(4,128)S(1)} async-done(((f32[16,2,4,128]{3,2,1,0:T(4,128)}), f32[16,2,4,128]{3,2,1,0:T(4,128)S(1)}, u32[]{:S(2)}, u32[]{:S(2)}) %all-to-all-start.1) | async-done | bytes 65568 | tf_op jit(solution)/shard_map/all_to_all | solution.py:59
  906.2 0.7 reshape.87
  (30 shorter events, 1.2 us)
Async XLA Ops:
  6.5 1.8 copy-start
  6.5 67.9 %copy-start.5 = (s32[32]{0:T(128)S(1)}, s32[32]{0:T(128)}, u32[]{:S(2)}) copy-start(s32[32]{0:T(128)} %param.13) | copy-start | bytes 388
  6.5 68.0 %copy-start.3 = (s32[32]{0:T(128)S(1)}, s32[32]{0:T(128)}, u32[]{:S(2)}) copy-start(s32[32]{0:T(128)} %param.10) | copy-start | bytes 388
  6.5 311.7 %copy-start.1 = (bf16[2,512,640]{2,1,0:T(8,128)(2,1)S(1)}, bf16[2,512,640]{2,1,0:T(8,128)(2,1)}, u32[]{:S(2)}) copy-start(bf16[2,512,640]{2,1,0:T(8,128)(2,1)} %param.9) | copy-start | bytes 3932164
  6.5 207.9 %all-gather.5.cloned.1.call-start = ((), (), s32[]{:S(2)}) async-start(), calls=%async_computation.3 | async-start | bytes 2162688 | tf_op jit(solution)/shard_map/all_gather | solution.py:39
  73.7 244.6 %all-gather.3.cloned.1.call-start = ((), (), s32[]{:S(2)}) async-start(), calls=%async_computation.2 | async-start | bytes 5570560 | tf_op jit(solution)/shard_map/all_gather | solution.py:40
  74.4 794.7 %all-reduce.2.cloned.1.call-start = ((), (), s32[]{:S(2)}) async-start(), calls=%async_computation.4 | async-start | bytes 262144 | tf_op jit(solution)/shard_map/psum | solution.py:52
  318.3 577.5 %copy-start.4 = (s32[32]{0:T(128)S(1)}, s32[32]{0:T(128)}, u32[]{:S(2)}) copy-start(s32[32]{0:T(128)} %param.11) | copy-start | bytes 388
  336.6 0.7 copy-start.2
  870.5 35.3 %all-to-all-start.1 = ((f32[16,2,4,128]{3,2,1,0:T(4,128)}), f32[16,2,4,128]{3,2,1,0:T(4,128)S(1)}, u32[]{:S(2)}, u32[]{:S(2)}) async-start(f32[16,2,4,128]{3,2,1,0:T(4,128)} %broadcast_multiply_fusion), calls=%async_computation.1 | async-start | bytes 131072 | tf_op jit(solution)/shard_map/all_to_all | solution.py:59
Sparse Core Ops, SparseCore 0:
  73.8 140.6 all-gather.4
  216.6 101.6 all-gather.2
  337.4 531.7 all-reduce.1
where the time goes:
time: 914 us; the launch traced here: 913 us
  waiting for transfers between devices  786 us (86%)
  blocking collectives  63.6 us (7%)
  starting transfers between devices  25.3 us (3%)
  between operations  13.2 us (1%)
  matrix products  13 us (1%)
    psum x1, waiting for transfers between devices, per_device(): summed = lax.psum(partial_value, 'aux')  532 us
    all_gather x1, waiting for transfers between devices, per_device(): full_rows = lax.all_gather(fetched, 'aux', axis=2, tiled=True)  140 us
    all_gather x1, waiting for transfers between devices, per_device(): segment = lax.all_gather(aux_factor, 'pair', axis=0, tiled=True)  104 us
    all_to_all x1, blocking collectives, per_device(): lax.all_to_all(picked, 'pair', split_axis=0, concat_axis=0, tiled=True)  63.6 us
    all_to_all x1, starting transfers between devices, per_device(): lax.all_to_all(outgoing, 'pair', split_axis=0, concat_axis=0, tiled=True)  25.2 us
  transfers between devices with their start and end apart: 4, of which 4 were waited for; matrix products, arithmetic and copies ran while one was open for 0% of the time, Pallas kernels for 0%

commit v1 on v0

v1 whole, which is shorter than its diff:
```python
import functools

import jax
import jax.numpy as jnp
from jax import lax
from jax.experimental import pallas as pl
from jax.experimental.pallas import tpu as pltpu
from jax.sharding import PartitionSpec as P

BLOCK_FUNCTIONS = 128
CORES = 2
HALVES = 2
ROW = 4
PIECES = 2
MESH = pl.DeviceIdType.MESH


def exchange_kernel(
    cols_ref,
    live_ref,
    ints_hbm,
    x_hbm,
    z_hbm,
    out_ref,
    zbuf,
    ibuf,
    xchip,
    xin,
    xout,
    xfull,
    tpart,
    trecv,
    sbuf,
    t2recv,
    fbuf,
    fin,
    local_sem,
    z_send,
    z_side,
    z_recv,
    xchip_send,
    xchip_recv,
    xr_send,
    xr_recv,
    xpeer_send,
    xpeer_recv,
    xg_send,
    xg_recv,
    t1_send,
    t1_recv,
    t2_send,
    t2_recv,
    t3_send,
    t3_recv,
):
    pairs = lax.axis_size("pair")
    auxes = lax.axis_size("aux")
    nz = pairs // CORES
    ny = auxes // (HALVES * ROW)
    plane = ny * ROW
    p = lax.axis_index("pair")
    j = lax.axis_index("aux")
    k = p // CORES
    c = p % CORES
    sib = p + 1 - 2 * c
    x = j % ROW
    half = (j // ROW) % HALVES
    y = j // (ROW * HALVES)
    peer = j + (1 - 2 * half) * ROW
    slots = ints_hbm.shape[0]
    blocks_own = x_hbm.shape[0]
    shard_rows = z_hbm.shape[0]
    piece_rows = shard_rows // PIECES
    chunks = shard_rows // BLOCK_FUNCTIONS
    width = BLOCK_FUNCTIONS
    mus = ints_hbm.shape[1] // width
    blocks_chip = CORES * blocks_own

    def aux_of(yy, hh, xx):
        return (yy * HALVES + hh) * ROW + xx

    def plane_aux(rel):
        return aux_of(lax.rem(y + rel // ROW, ny), half, lax.rem(x + rel % ROW, ROW))

    barrier = pltpu.get_barrier_semaphore()

    def greet_line(rel, _):
        pl.semaphore_signal(
            barrier, inc=1, device_id=(lax.rem(p + rel, pairs), j), device_id_type=MESH
        )
        return 0

    lax.fori_loop(1, pairs, greet_line, 0)

    def greet_plane(rel, _):
        pl.semaphore_signal(barrier, inc=1, device_id=(p, plane_aux(rel)), device_id_type=MESH)
        return 0

    lax.fori_loop(1, plane, greet_plane, 0)
    pl.semaphore_signal(barrier, inc=1, device_id=(p, peer), device_id_type=MESH)

    load_i = pltpu.make_async_copy(ints_hbm, ibuf, local_sem.at[0])
    load_z = pltpu.make_async_copy(z_hbm, zbuf.at[p], local_sem.at[1])
    own_x = xchip.at[pl.ds(c * blocks_own, blocks_own)]
    load_x = pltpu.make_async_copy(x_hbm, own_x, local_sem.at[2])
    load_x.start()
    load_z.start()
    load_i.start()
    pl.semaphore_wait(barrier, pairs - 1 + plane - 1 + 1)

    def z_copy(direction, shard_chip, piece, own=False):
        rows = pl.ds(piece * piece_rows, piece_rows)
        shard = shard_chip * CORES + c
        src = z_hbm.at[rows] if own else zbuf.at[shard, rows]
        target = p + CORES if direction == 0 else p - CORES
        return pltpu.make_async_remote_copy(
            src_ref=src,
            dst_ref=zbuf.at[shard, rows],
            send_sem=z_send.at[direction, shard_chip, piece],
            recv_sem=z_recv.at[shard, piece],
            device_id=(target, j),
            device_id_type=MESH,
        )

    def z_side_copy(shard_chip, piece, own=False):
        rows = pl.ds(piece * piece_rows, piece_rows)
        shard = shard_chip * CORES + c
        src = z_hbm.at[rows] if own else zbuf.at[shard, rows]
        return pltpu.make_async_remote_copy(
            src_ref=src,
            dst_ref=zbuf.at[shard, rows],
            send_sem=z_side.at[0],
            recv_sem=z_recv.at[shard, piece],
            device_id=(sib, j),
            device_id_type=MESH,
        )

    def z_arrived(shard, piece):
        rows = pl.ds(piece * piece_rows, piece_rows)
        pltpu.make_async_copy(
            zbuf.at[shard, rows], zbuf.at[shard, rows], z_recv.at[shard, piece]
        ).wait()

    x_side = pltpu.make_async_remote_copy(
        src_ref=x_hbm,
        dst_ref=own_x,
        send_sem=xchip_send.at[0],
        recv_sem=xchip_recv.at[0],
        device_id=(sib, j),
        device_id_type=MESH,
    )
    x_side.start()
    for piece in range(PIECES):

        @pl.when(k < nz - 1)
        def _():
            z_copy(0, k, piece, own=True).start()

        @pl.when(k > 0)
        def _():
            z_copy(1, k, piece, own=True).start()

    for piece in range(PIECES):
        z_side_copy(k, piece, own=True).start()

    load_x.wait()
    pltpu.make_async_copy(own_x, own_x, xchip_recv.at[0]).wait()

    def picked(dest, slot):
        number = (dest * CORES + c) * slots + slot
        local = cols_ref[number] - k * blocks_chip
        near = jnp.minimum(jnp.maximum(local, 0), blocks_chip - 1)
        here = (near == local).astype(jnp.float32)
        return xchip[near].astype(jnp.float32) * here

    def x_copy(direction, dest):
        target = p + CORES if direction == 0 else p - CORES
        return pltpu.make_async_remote_copy(
            src_ref=xout.at[dest],
            dst_ref=xin.at[direction, dest],
            send_sem=xr_send.at[direction, dest],
            recv_sem=xr_recv.at[direction, dest],
            device_id=(target, j),
            device_id_type=MESH,
        )

    def x_arrived(direction, dest):
        pltpu.make_async_copy(
            xin.at[direction, dest], xin.at[direction, dest], xr_recv.at[direction, dest]
        ).wait()

    def x_step(tau, _):
        for direction in range(2):
            place = k if direction == 0 else nz - 1 - k
            far = nz - 1 - tau + place
            dest = far if direction == 0 else nz - 1 - far

            @pl.when(place <= tau)
            def _():
                @pl.when(place > 0)
                def _():
                    x_arrived(direction, dest)
                    for slot in range(slots):
                        got = xin[direction, dest, slot].astype(jnp.float32)
                        xout[dest, slot] = (picked(dest, slot) + got).astype(xout.dtype)

                @pl.when(place == 0)
                def _():
                    for slot in range(slots):
                        xout[dest, slot] = picked(dest, slot).astype(xout.dtype)

                x_copy(direction, dest).start()

        return 0

    lax.fori_loop(0, nz - 1, x_step, 0)

    for slot in range(slots):
        xout[k, slot] = picked(k, slot).astype(xout.dtype)

    @pl.when(k > 0)
    def _():
        x_arrived(0, k)
        for slot in range(slots):
            total = xout[k, slot].astype(jnp.float32) + xin[0, k, slot].astype(jnp.float32)
            xout[k, slot] = total.astype(xout.dtype)

    @pl.when(k < nz - 1)
    def _():
        x_arrived(1, k)
        for slot in range(slots):
            total = xout[k, slot].astype(jnp.float32) + xin[1, k, slot].astype(jnp.float32)
            xout[k, slot] = total.astype(xout.dtype)

    xfull[j] = xout[k]

    x_peer = pltpu.make_async_remote_copy(
        src_ref=xout.at[k],
        dst_ref=xfull.at[j],
        send_sem=xpeer_send.at[0],
        recv_sem=xpeer_recv.at[0],
        device_id=(p, peer),
        device_id_type=MESH,
    )
    x_peer.start()

    def x_plane(which):
        def body(rel, _):
            pltpu.make_async_remote_copy(
                src_ref=xfull.at[which],
                dst_ref=xfull.at[which],
                send_sem=xg_send.at[0],
                recv_sem=xg_recv.at[0],
                device_id=(p, plane_aux(rel)),
                device_id_type=MESH,
            ).start()
            return 0

        lax.fori_loop(1, plane, body, 0)

    x_plane(j)

    def contract(shard):
        z = zbuf[shard]
        for slot in range(slots):
            products = lax.dot_general(
                ibuf[slot], z, (((1,), (1,)), ((), ())), preferred_element_type=jnp.float32
            )
            alive = live_ref[p * slots + slot].astype(jnp.float32)
            for h in range(chunks):
                chunk = shard * chunks + h
                rows = xfull[chunk, slot].astype(jnp.float32)
                part = products[:, h * width : (h + 1) * width].reshape(mus, width, width)
                term = jnp.sum(part * rows[None], axis=1) * alive
                tpart[chunk, slot * mus : (slot + 1) * mus, :] = term
        for h in range(chunks):
            chunk = shard * chunks + h
            yy = chunk // (HALVES * ROW)
            hh = (chunk // ROW) % HALVES
            xx = chunk % ROW
            rel = lax.rem(y - yy + ny, ny) * ROW + lax.rem(x - xx + ROW, ROW)

            @pl.when(rel > 0)
            def _():
                pltpu.make_async_remote_copy(
                    src_ref=tpart.at[chunk],
                    dst_ref=trecv.at[rel - 1, hh],
                    send_sem=t1_send.at[0],
                    recv_sem=t1_recv.at[0],
                    device_id=(p, aux_of(yy, half, xx)),
                    device_id_type=MESH,
                ).start()

    def contract_set(step):
        def one(n, _):
            direction = n // CORES
            core = lax.rem(c + n, CORES)
            chip = jnp.where(direction == 0, k - step, k + step)
            shard = chip * CORES + core
            valid = jnp.logical_and(chip >= 0, chip < nz)
            valid = jnp.logical_and(valid, jnp.logical_or(step > 0, direction == 0))

            @pl.when(valid)
            def _():
                @pl.when(core != c)
                def _():
                    for piece in range(PIECES):
                        z_arrived(shard, piece)

                contract(shard)

            return 0

        lax.fori_loop(0, 2 * CORES, one, 0)

    load_z.wait()
    load_i.wait()

    first = nz // 2 + 1

    def z_step(t, _):
        for piece in range(PIECES):

            @pl.when(k - t >= 0)
            def _():
                z_arrived((k - t) * CORES + c, piece)

                @pl.when(k < nz - 1)
                def _():
                    z_copy(0, k - t, piece).start()

                z_side_copy(k - t, piece).start()

            @pl.when(k + t < nz)
            def _():
                z_arrived((k + t) * CORES + c, piece)

                @pl.when(k > 0)
                def _():
                    z_copy(1, k + t, piece).start()

                z_side_copy(k + t, piece).start()

        @pl.when(t == 1)
        def _():
            pltpu.make_async_copy(xfull.at[0], xfull.at[0], xpeer_recv.at[0]).wait()
            x_plane(peer)

        @pl.when(t == first)
        def _():
            everything = xfull.at[pl.ds(0, HALVES * (plane - 1))]
            pltpu.make_async_copy(everything, everything, xg_recv.at[0]).wait()

        @pl.when(t >= first)
        def _():
            contract_set(2 * (t - first))
            contract_set(2 * (t - first) + 1)

        return 0

    lax.fori_loop(1, 2 * first - 1, z_step, 0)

    pltpu.make_async_copy(trecv, trecv, t1_recv.at[0]).wait()
    mine = jnp.sum(trecv[:, half], axis=0) + tpart[aux_of(y, half, x)]
    theirs = jnp.sum(trecv[:, 1 - half], axis=0) + tpart[aux_of(y, 1 - half, x)]
    sbuf[...] = theirs
    t2 = pltpu.make_async_remote_copy(
        src_ref=sbuf,
        dst_ref=t2recv,
        send_sem=t2_send.at[0],
        recv_sem=t2_recv.at[0],
        device_id=(p, peer),
        device_id_type=MESH,
    )
    t2.start()
    t2.wait_recv()
    final = mine + t2recv[...]
    fbuf[...] = final
    out_ref[p] = final

    def spread(rel, _):
        pltpu.make_async_remote_copy(
            src_ref=fbuf,
            dst_ref=fin.at[pairs - 1 - rel],
            send_sem=t3_send.at[0],
            recv_sem=t3_recv.at[0],
            device_id=(lax.rem(p + rel, pairs), j),
            device_id_type=MESH,
        ).start()
        return 0

    lax.fori_loop(1, pairs, spread, 0)
    pltpu.make_async_copy(fin, fin, t3_recv.at[0]).wait()

    def take(rel, _):
        out_ref[lax.rem(p + rel, pairs)] = fin[rel - 1]
        return 0

    lax.fori_loop(1, pairs, take, 0)

    x_side.wait_send()
    x_peer.wait_send()
    t2.wait_send()
    pltpu.make_async_copy(fin, fin, t3_send.at[0]).wait()
    pltpu.make_async_copy(trecv, trecv, t1_send.at[0]).wait()
    sent = xfull.at[pl.ds(0, HALVES * (plane - 1))]
    pltpu.make_async_copy(sent, sent, xg_send.at[0]).wait()
    sent_z = zbuf.at[pl.ds(0, nz)]
    pltpu.make_async_copy(sent_z, sent_z, z_side.at[0]).wait()

    def z_sent(chip, _):
        @pl.when(jnp.logical_and(chip <= k, k < nz - 1))
        def _():
            for piece in range(PIECES):
                z_copy(0, chip, piece).wait_send()

        @pl.when(jnp.logical_and(chip >= k, k > 0))
        def _():
            for piece in range(PIECES):
                z_copy(1, chip, piece).wait_send()

        @pl.when(chip > k)
        def _():
            x_copy(0, chip).wait_send()

        @pl.when(chip < k)
        def _():
            x_copy(1, chip).wait_send()

        return 0

    lax.fori_loop(0, nz, z_sent, 0)


def place_kernel(first_block, blocks_dev, strips, slots, rows_ref, strip_ref, sums_ref, out_ref):
    out_ref[...] = jnp.zeros_like(out_ref)
    base = first_block[0]
    rows, columns = sums_ref.shape[1:]
    mus = rows // slots
    sublane = lax.broadcasted_iota(jnp.int32, (rows, columns), 0) // mus

    def body(p, _):
        value = sums_ref[p]
        turned = pltpu.roll(value, mus, 0)
        for slot in range(slots):
            number = p * slots + slot
            local = rows_ref[number] - base
            strip = local * strips + strip_ref[number]
            part = strip % slots
            tile = strip // slots

            @pl.when(jnp.logical_and(local >= 0, local < blocks_dev))
            def _():
                moved = jnp.where(part == slot, value, turned)
                kept = jnp.where(sublane == part, moved, 0.0)
                at = pl.ds(pl.multiple_of(tile * rows, rows), rows)
                out_ref[at, :] = out_ref[at, :] + kept

        return 0

    lax.fori_loop(0, sums_ref.shape[0], body, 0)


def per_device(
    integral_strips,
    slot_row_block,
    slot_strip_index,
    slot_column_block,
    block_live,
    ao_factor,
    aux_factor,
):
    slots, strip_size, depth = integral_strips.shape
    width = BLOCK_FUNCTIONS
    mus = strip_size // width
    pairs = lax.axis_size("pair")
    auxes = lax.axis_size("aux")
    nz = pairs // CORES
    plane = auxes // HALVES
    shard_rows = aux_factor.shape[0]
    rows_x, rank_part = ao_factor.shape
    blocks_dev = rows_x // width
    x_blocks = ao_factor.reshape(blocks_dev, width, rank_part)
    smem = pl.BlockSpec(memory_space=pltpu.SMEM)
    hbm = pl.BlockSpec(memory_space=pl.ANY)
    vmem = pl.BlockSpec(memory_space=pltpu.VMEM)
    rows = slots * mus
    dma = pltpu.SemaphoreType.DMA
    sums = pl.pallas_call(
        exchange_kernel,
        out_shape=jax.ShapeDtypeStruct((pairs, rows, rank_part), jnp.float32),
        in_specs=[smem, smem, hbm, hbm, hbm],
        out_specs=vmem,
        scratch_shapes=[
            pltpu.VMEM((pairs, shard_rows, depth), jnp.bfloat16),
            pltpu.VMEM((slots, strip_size, depth), jnp.bfloat16),
            pltpu.VMEM((CORES * blocks_dev, width, rank_part), jnp.bfloat16),
            pltpu.VMEM((2, nz, slots, width, rank_part), jnp.bfloat16),
            pltpu.VMEM((nz, slots, width, rank_part), jnp.bfloat16),
            pltpu.VMEM((auxes, slots, width, rank_part), jnp.bfloat16),
            pltpu.VMEM((auxes, rows, rank_part), jnp.float32),
            pltpu.VMEM((plane - 1, HALVES, rows, rank_part), jnp.float32),
            pltpu.VMEM((rows, rank_part), jnp.float32),
            pltpu.VMEM((rows, rank_part), jnp.float32),
            pltpu.VMEM((rows, rank_part), jnp.float32),
            pltpu.VMEM((pairs - 1, rows, rank_part), jnp.float32),
            dma((3,)),
            dma((2, nz, PIECES)),
            dma((1,)),
            dma((pairs, PIECES)),
            dma((1,)),
            dma((1,)),
            dma((2, nz)),
            dma((2, nz)),
            dma((1,)),
            dma((1,)),
            dma((1,)),
            dma((1,)),
            dma((1,)),
            dma((1,)),
            dma((1,)),
            dma((1,)),
            dma((1,)),
            dma((1,)),
        ],
        compiler_params=pltpu.CompilerParams(
            collective_id=0, has_side_effects=True, vmem_limit_bytes=40 * 2**20
        ),
        name="exchange",
    )(slot_column_block, block_live, integral_strips, x_blocks, aux_factor)

    first_block = (lax.axis_index("pair") * blocks_dev).astype(jnp.int32).reshape(1)
    return pl.pallas_call(
        lambda base, *refs: place_kernel(base, blocks_dev, width // mus, slots, *refs),
        out_shape=jax.ShapeDtypeStruct((rows_x, rank_part), jnp.float32),
        in_specs=[smem, smem, smem, vmem],
        out_specs=vmem,
        name="place",
    )(first_block, slot_row_block, slot_strip_index, sums)


def solution(mesh):
    in_specs = (P("pair", None, "aux"), P(), P(), P(), P(), P("pair", "aux"), P("pair", "aux"))
    out_specs = P("pair", "aux")
    return jax.shard_map(
        per_device, mesh=mesh, in_specs=in_specs, out_specs=out_specs, check_vma=False
    )
```

time: 914 us -> 125 us (0.14)
  waiting for transfers between devices: 786 us -> 0 us
  Pallas kernels: 0 us -> 120 us
  blocking collectives: 63.6 us -> 0 us
  starting transfers between devices: 25.3 us -> 0 us
  between operations: 13.2 us -> 0.02 us
  matrix products: 13 us -> 0 us
    psum x1 -> x0, waiting for transfers between devices: 532 us -> none  [per_device(): summed = lax.psum(partial_value, 'aux')]
    all_gather x2 -> x0, waiting for transfers between devices: 244 us -> none  [the longest x1 140 us: per_device(): full_rows = lax.all_gather(fetched, 'aux', axis=2, tiled=True)]
    pallas_call x0 -> x2, Pallas kernels: none -> 120 us  [the longest x1 118 us: per_device(): pl.pallas_call(exchange_kernel, out_shape=jax.ShapeDtypeStruct((pairs, ro...]
    all_to_all x1 -> x0, blocking collectives: 63.6 us -> none  [per_device(): lax.all_to_all(picked, 'pair', split_axis=0, concat_axis=0, tiled=True)]
    all_to_all x1 -> x0, starting transfers between devices: 25.2 us -> none  [per_device(): lax.all_to_all(outgoing, 'pair', split_axis=0, concat_axis=0, tiled=True)]
    dot_general x3 -> x0, matrix products: 13 us -> none  [the longest x2 12.7 us: per_slot(): lax.dot_general(integrals, segment, (((1,), (1,)), ((), ())), preferred_e...]
    all_to_all x1 -> x0, waiting for transfers between devices: 10.1 us -> none  [per_device(): lax.all_to_all(outgoing, 'pair', split_axis=0, concat_axis=0, tiled=True)]
  transfers between devices with their start and end apart: 4 -> 0, of which waited for: 4 -> 0; matrix products, arithmetic and copies ran while one was open for 0% -> 0% of each run, Pallas kernels for 0% -> 0%
where the time goes in v1:
time: 125 us
  Pallas kernels  120 us (96%)
  local copies, waits for them, and re-layouts  5.1 us (4%)
    pallas_call x1, Pallas kernels, per_device(): pl.pallas_call(exchange_kernel, out_shape=jax.ShapeDtypeStruct((pairs, ro...  118 us
    unnamed x12, local copies, waits for them, and re-layouts  5.1 us

profile of v1, /device:TPU:1, one launch (start us, length us, event | category | flops | bytes accessed | tf_op | source)
XLA Modules:
  0.0 125.0 jit_solution(12256485587021627268)
XLA Ops:
  0.0 0.0 copy-start
  0.0 1.3 %copy-done = bf16[2,512,640]{2,1,0:T(8,128)(2,1)S(1)} copy-done((bf16[2,512,640]{2,1,0:T(8,128)(2,1)S(1)}, bf16[2,512,640]{2,1,0:T(8,128)(2,1)}, u32[]{:S(2)}) %copy-start) | copy-done | bytes 1310744
  1.3 0.0 copy-start.1
  1.3 1.0 copy-done.1
  2.3 0.0 copy-start.3
  2.3 0.9 copy-done.3
  3.2 0.0 copy-start.4
  3.2 0.7 copy-done.4
  3.8 0.0 copy-start.5
  3.8 0.7 copy-done.5
  4.5 117.7 %exchange.1.refs_2_ = f32[16,8,128]{2,1,0:T(8,128)S(1)} custom-call(s32[32]{0:T(128)S(1)} %copy-done.4, s32[32]{0:T(128)S(1)} %copy-done.5, bf16[2,512,640]{2,1,0:T(8,128)(2,1)S(1)} %copy-done, bf16[3,128,128]{2,1,0:T(8,128)(2,1)S(1)} %bitcast.2, bf16[256,640]{1,0:T(8,128)(2,1)S(1)} %copy-done.1), custom_call_target="tpu_custom_call" | custom-call | tf_op jit(solution)/shard_map/exchange/pallas_call | solution.py:489
  122.2 0.0 copy-start.2
  122.2 0.6 copy-done.2
  122.9 2.1 %place.1 = f32[384,128]{1,0:T(8,128)} custom-call(s32[1]{0:T(128)} %bitcast.base, s32[32]{0:T(128)} %refs_0_.1, s32[32]{0:T(128)} %refs_1_.1, f32[16,8,128]{2,1,0:T(8,128)} %copy-done.2), custom_call_target="tpu_custom_call" | custom-call | tf_op jit(solution)/shard_map/place/pallas_call | solution.py:533
Async XLA Ops:
  0.0 1.3 %copy-start = (bf16[2,512,640]{2,1,0:T(8,128)(2,1)S(1)}, bf16[2,512,640]{2,1,0:T(8,128)(2,1)}, u32[]{:S(2)}) copy-start(bf16[2,512,640]{2,1,0:T(8,128)(2,1)} %ints_hbm.1) | copy-start | bytes 3932164
  1.3 1.0 copy-start.1
  2.3 0.9 copy-start.3
  3.2 0.7 copy-start.4
  3.8 0.7 copy-start.5
  122.2 0.6 copy-start.2

commit v2 on v1

--- a/solution.py
+++ b/solution.py
@@ -12,16 +12,21 @@
 HALVES = 2
 ROW = 4
 PIECES = 2
+LEAD = 3
+EVENTS = {8: (11, 11, 11, 12, 12, 12, 12, 13), 4: (1, 2, 3, 5), 2: (1, 1)}
+PEER_LAG = 6
 MESH = pl.DeviceIdType.MESH
 
 
 def exchange_kernel(
-    cols_ref,
-    live_ref,
+    cols_hbm,
+    live_hbm,
     ints_hbm,
     x_hbm,
     z_hbm,
     out_ref,
+    cols_ref,
+    live_ref,
     zbuf,
     ibuf,
     xchip,
@@ -31,8 +36,6 @@
     tpart,
     trecv,
     sbuf,
-    t2recv,
-    fbuf,
     fin,
     local_sem,
     z_send,
@@ -50,8 +53,6 @@
     t1_recv,
     t2_send,
     t2_recv,
-    t3_send,
-    t3_recv,
 ):
     pairs = lax.axis_size("pair")
     auxes = lax.axis_size("aux")
@@ -97,19 +98,30 @@
         return 0
 
     lax.fori_loop(1, plane, greet_plane, 0)
-    pl.semaphore_signal(barrier, inc=1, device_id=(p, peer), device_id_type=MESH)
+
+    def greet_peers(rel, _):
+        pl.semaphore_signal(
+            barrier, inc=1, device_id=(lax.rem(p + rel, pairs), peer), device_id_type=MESH
+        )
+        return 0
+
+    lax.fori_loop(0, pairs, greet_peers, 0)
 
     load_i = pltpu.make_async_copy(ints_hbm, ibuf, local_sem.at[0])
     load_z = pltpu.make_async_copy(z_hbm, zbuf.at[p], local_sem.at[1])
     own_x = xchip.at[pl.ds(c * blocks_own, blocks_own)]
     load_x = pltpu.make_async_copy(x_hbm, own_x, local_sem.at[2])
+    load_cols = pltpu.make_async_copy(cols_hbm, cols_ref, local_sem.at[3])
+    load_live = pltpu.make_async_copy(live_hbm, live_ref, local_sem.at[4])
     load_x.start()
+    load_cols.start()
+    load_live.start()
     load_z.start()
     load_i.start()
-    pl.semaphore_wait(barrier, pairs - 1 + plane - 1 + 1)
+    pl.semaphore_wait(barrier, 2 * pairs - 1 + plane - 1)
 
     def z_copy(direction, shard_chip, piece, own=False):
-        rows = pl.ds(piece * piece_rows, piece_rows)
+        rows = pl.ds(pl.multiple_of(piece * piece_rows, piece_rows), piece_rows)
         shard = shard_chip * CORES + c
         src = z_hbm.at[rows] if own else zbuf.at[shard, rows]
         target = p + CORES if direction == 0 else p - CORES
@@ -123,7 +135,7 @@
         )
 
     def z_side_copy(shard_chip, piece, own=False):
-        rows = pl.ds(piece * piece_rows, piece_rows)
+        rows = pl.ds(pl.multiple_of(piece * piece_rows, piece_rows), piece_rows)
         shard = shard_chip * CORES + c
         src = z_hbm.at[rows] if own else zbuf.at[shard, rows]
         return pltpu.make_async_remote_copy(
@@ -136,7 +148,7 @@
         )
 
     def z_arrived(shard, piece):
-        rows = pl.ds(piece * piece_rows, piece_rows)
+        rows = pl.ds(pl.multiple_of(piece * piece_rows, piece_rows), piece_rows)
         pltpu.make_async_copy(
             zbuf.at[shard, rows], zbuf.at[shard, rows], z_recv.at[shard, piece]
         ).wait()
@@ -164,6 +176,8 @@
         z_side_copy(k, piece, own=True).start()
 
     load_x.wait()
+    load_cols.wait()
+    load_live.wait()
     pltpu.make_async_copy(own_x, own_x, xchip_recv.at[0]).wait()
 
     def picked(dest, slot):
@@ -213,26 +227,8 @@
 
         return 0
 
-    lax.fori_loop(0, nz - 1, x_step, 0)
-
-    for slot in range(slots):
-        xout[k, slot] = picked(k, slot).astype(xout.dtype)
-
-    @pl.when(k > 0)
-    def _():
-        x_arrived(0, k)
-        for slot in range(slots):
-            total = xout[k, slot].astype(jnp.float32) + xin[0, k, slot].astype(jnp.float32)
-            xout[k, slot] = total.astype(xout.dtype)
-
-    @pl.when(k < nz - 1)
-    def _():
-        x_arrived(1, k)
-        for slot in range(slots):
-            total = xout[k, slot].astype(jnp.float32) + xin[1, k, slot].astype(jnp.float32)
-            xout[k, slot] = total.astype(xout.dtype)
-
-    xfull[j] = xout[k]
+    lead = min(LEAD, nz - 1)
+    lax.fori_loop(0, lead, x_step, 0)
 
     x_peer = pltpu.make_async_remote_copy(
         src_ref=xout.at[k],
@@ -242,15 +238,35 @@
         device_id=(p, peer),
         device_id_type=MESH,
     )
-    x_peer.start()
-
-    def x_plane(which):
+
+    def x_last():
+        for slot in range(slots):
+            xout[k, slot] = picked(k, slot).astype(xout.dtype)
+
+        @pl.when(k > 0)
+        def _():
+            x_arrived(0, k)
+            for slot in range(slots):
+                total = xout[k, slot].astype(jnp.float32) + xin[0, k, slot].astype(jnp.float32)
+                xout[k, slot] = total.astype(xout.dtype)
+
+        @pl.when(k < nz - 1)
+        def _():
+            x_arrived(1, k)
+            for slot in range(slots):
+                total = xout[k, slot].astype(jnp.float32) + xin[1, k, slot].astype(jnp.float32)
+                xout[k, slot] = total.astype(xout.dtype)
+
+        xfull[j] = xout[k]
+        x_peer.start()
+
+    def x_plane(which, which_half):
         def body(rel, _):
             pltpu.make_async_remote_copy(
                 src_ref=xfull.at[which],
                 dst_ref=xfull.at[which],
-                send_sem=xg_send.at[0],
-                recv_sem=xg_recv.at[0],
+                send_sem=xg_send.at[which_half],
+                recv_sem=xg_recv.at[which_half],
                 device_id=(p, plane_aux(rel)),
                 device_id_type=MESH,
             ).start()
@@ -258,7 +274,9 @@
 
         lax.fori_loop(1, plane, body, 0)
 
-    x_plane(j)
+    def x_plane_arrived(which_half):
+        some = xfull.at[pl.ds(0, plane - 1)]
+        pltpu.make_async_copy(some, some, xg_recv.at[which_half]).wait()
 
     def contract(shard):
         z = zbuf[shard]
@@ -284,9 +302,9 @@
             def _():
                 pltpu.make_async_remote_copy(
                     src_ref=tpart.at[chunk],
-                    dst_ref=trecv.at[rel - 1, hh],
+                    dst_ref=trecv.at[hh, rel - 1],
                     send_sem=t1_send.at[0],
-                    recv_sem=t1_recv.at[0],
+                    recv_sem=t1_recv.at[hh],
                     device_id=(p, aux_of(yy, half, xx)),
                     device_id_type=MESH,
                 ).start()
@@ -316,95 +334,134 @@
     load_z.wait()
     load_i.wait()
 
-    first = nz // 2 + 1
-
-    def z_step(t, _):
-        for piece in range(PIECES):
-
-            @pl.when(k - t >= 0)
+    done_at = EVENTS[nz]
+    early = nz // 2 - 1
+    own_parity = lax.rem(half + k, 2)
+
+    def step_of(item):
+        own = own_parity + 2 * item
+        other = 1 - own_parity + 2 * (item - early)
+        return jnp.where(item < early, own, jnp.where(item < 2 * early, other, item))
+
+    def item_of(step):
+        own = lax.rem(step + own_parity, 2) == 0
+        listed = jnp.where(own, (step - own_parity) // 2, early + (step - 1 + own_parity) // 2)
+        return jnp.where(step < 2 * early, listed, step)
+
+    def finished_at(item):
+        event = jnp.int32(done_at[0])
+        for n in range(1, nz):
+            event = jnp.where(item >= n, done_at[n], event)
+        return event
+
+    def items_by(event):
+        count = jnp.int32(0)
+        for n in range(nz):
+            count = count + (event >= done_at[n]).astype(jnp.int32)
+        return count
+
+    last_event = 2 * (nz - 1)
+    x_event = nz - 1 - lead
+    peer_event = min(x_event + PEER_LAG, done_at[early])
+
+    def spread(hh):
+        pltpu.make_async_copy(trecv.at[hh], trecv.at[hh], t1_recv.at[hh]).wait()
+        sbuf[hh] = jnp.sum(trecv[hh], axis=0) + tpart[aux_of(y, hh, x)]
+        near = jnp.where(half == hh, 1, 0)
+
+        def send(rel, _):
+            slot = jnp.where(half == hh, pairs - 1 - rel, pairs - 1 + lax.rem(pairs - rel, pairs))
+            pltpu.make_async_remote_copy(
+                src_ref=sbuf.at[hh],
+                dst_ref=fin.at[slot],
+                send_sem=t2_send.at[0],
+                recv_sem=t2_recv.at[0],
+                device_id=(lax.rem(p + rel, pairs), aux_of(y, hh, x)),
+                device_id_type=MESH,
+            ).start()
+            return 0
+
+        lax.fori_loop(near, pairs, send, 0)
+
+    def event_step(event, _):
+        t = event // 2 + 1
+        piece = lax.rem(event, 2)
+
+        @pl.when(k - t >= 0)
+        def _():
+            z_arrived((k - t) * CORES + c, piece)
+
+            @pl.when(k < nz - 1)
             def _():
-                z_arrived((k - t) * CORES + c, piece)
-
-                @pl.when(k < nz - 1)
-                def _():
-                    z_copy(0, k - t, piece).start()
-
-                z_side_copy(k - t, piece).start()
-
-            @pl.when(k + t < nz)
+                z_copy(0, k - t, piece).start()
+
+            z_side_copy(k - t, piece).start()
+
+        @pl.when(k + t < nz)
+        def _():
+            z_arrived((k + t) * CORES + c, piece)
+
+            @pl.when(k > 0)
             def _():
-                z_arrived((k + t) * CORES + c, piece)
-
-                @pl.when(k > 0)
-                def _():
-                    z_copy(1, k + t, piece).start()
-
-                z_side_copy(k + t, piece).start()
-
-        @pl.when(t == 1)
+                z_copy(1, k + t, piece).start()
+
+            z_side_copy(k + t, piece).start()
+
+        @pl.when(event < x_event)
+        def _():
+            x_step(event + lead, 0)
+
+        @pl.when(event == x_event)
+        def _():
+            x_last()
+            x_plane(j, 0)
+
+        @pl.when(event == peer_event)
         def _():
             pltpu.make_async_copy(xfull.at[0], xfull.at[0], xpeer_recv.at[0]).wait()
-            x_plane(peer)
-
-        @pl.when(t == first)
-        def _():
-            everything = xfull.at[pl.ds(0, HALVES * (plane - 1))]
-            pltpu.make_async_copy(everything, everything, xg_recv.at[0]).wait()
-
-        @pl.when(t >= first)
-        def _():
-            contract_set(2 * (t - first))
-            contract_set(2 * (t - first) + 1)
-
-        return 0
-
-    lax.fori_loop(1, 2 * first - 1, z_step, 0)
-
-    pltpu.make_async_copy(trecv, trecv, t1_recv.at[0]).wait()
-    mine = jnp.sum(trecv[:, half], axis=0) + tpart[aux_of(y, half, x)]
-    theirs = jnp.sum(trecv[:, 1 - half], axis=0) + tpart[aux_of(y, 1 - half, x)]
-    sbuf[...] = theirs
-    t2 = pltpu.make_async_remote_copy(
-        src_ref=sbuf,
-        dst_ref=t2recv,
-        send_sem=t2_send.at[0],
-        recv_sem=t2_recv.at[0],
-        device_id=(p, peer),
-        device_id_type=MESH,
-    )
-    t2.start()
-    t2.wait_recv()
-    final = mine + t2recv[...]
-    fbuf[...] = final
-    out_ref[p] = final
-
-    def spread(rel, _):
-        pltpu.make_async_remote_copy(
-            src_ref=fbuf,
-            dst_ref=fin.at[pairs - 1 - rel],
-            send_sem=t3_send.at[0],
-            recv_sem=t3_recv.at[0],
-            device_id=(lax.rem(p + rel, pairs), j),
-            device_id_type=MESH,
-        ).start()
-        return 0
-
-    lax.fori_loop(1, pairs, spread, 0)
-    pltpu.make_async_copy(fin, fin, t3_recv.at[0]).wait()
+            x_plane(peer, 1)
+
+        @pl.when(event == done_at[0])
+        def _():
+            x_plane_arrived(0)
+
+        @pl.when(event == done_at[early])
+        def _():
+            x_plane_arrived(1)
+
+        for hh in range(HALVES):
+            step = jnp.abs(k - aux_of(y, hh, x) // (chunks * CORES))
+
+            @pl.when(event == finished_at(item_of(step)) + 1)
+            def _():
+                spread(hh)
+
+        def work(item, _):
+            contract_set(step_of(item))
+            return 0
+
+        lax.fori_loop(items_by(event - 1), items_by(event), work, 0)
+
+        return 0
+
+    lax.fori_loop(0, last_event + 1, event_step, 0)
+
+    pltpu.make_async_copy(fin, fin, t2_recv.at[0]).wait()
+    out_ref[p] = sbuf[half] + fin[pairs - 1]
 
     def take(rel, _):
-        out_ref[lax.rem(p + rel, pairs)] = fin[rel - 1]
+        out_ref[lax.rem(p + rel, pairs)] = fin[rel - 1] + fin[pairs - 1 + rel]
         return 0
 
     lax.fori_loop(1, pairs, take, 0)
 
     x_side.wait_send()
     x_peer.wait_send()
-    t2.wait_send()
-    pltpu.make_async_copy(fin, fin, t3_send.at[0]).wait()
+    pltpu.make_async_copy(fin, fin, t2_send.at[0]).wait()
     pltpu.make_async_copy(trecv, trecv, t1_send.at[0]).wait()
-    sent = xfull.at[pl.ds(0, HALVES * (plane - 1))]
-    pltpu.make_async_copy(sent, sent, xg_send.at[0]).wait()
+    sent = xfull.at[pl.ds(0, plane - 1)]
+    for which in range(HALVES):
+        pltpu.make_async_copy(sent, sent, xg_send.at[which]).wait()
     sent_z = zbuf.at[pl.ds(0, nz)]
     pltpu.make_async_copy(sent_z, sent_z, z_side.at[0]).wait()
 
@@ -482,16 +539,18 @@
     blocks_dev = rows_x // width
     x_blocks = ao_factor.reshape(blocks_dev, width, rank_part)
     smem = pl.BlockSpec(memory_space=pltpu.SMEM)
-    hbm = pl.BlockSpec(memory_space=pl.ANY)
+    hbm = pl.BlockSpec(memory_space=pltpu.HBM)
     vmem = pl.BlockSpec(memory_space=pltpu.VMEM)
     rows = slots * mus
     dma = pltpu.SemaphoreType.DMA
     sums = pl.pallas_call(
         exchange_kernel,
         out_shape=jax.ShapeDtypeStruct((pairs, rows, rank_part), jnp.float32),
-        in_specs=[smem, smem, hbm, hbm, hbm],
+        in_specs=[hbm, hbm, hbm, hbm, hbm],
         out_specs=vmem,
         scratch_shapes=[
+            pltpu.SMEM((slot_column_block.shape[0],), jnp.int32),
+            pltpu.SMEM((block_live.shape[0],), jnp.int32),
             pltpu.VMEM((pairs, shard_rows, depth), jnp.bfloat16),
             pltpu.VMEM((slots, strip_size, depth), jnp.bfloat16),
             pltpu.VMEM((CORES * blocks_dev, width, rank_part), jnp.bfloat16),
@@ -499,12 +558,10 @@
             pltpu.VMEM((nz, slots, width, rank_part), jnp.bfloat16),
             pltpu.VMEM((auxes, slots, width, rank_part), jnp.bfloat16),
             pltpu.VMEM((auxes, rows, rank_part), jnp.float32),
-            pltpu.VMEM((plane - 1, HALVES, rows, rank_part), jnp.float32),
-            pltpu.VMEM((rows, rank_part), jnp.float32),
-            pltpu.VMEM((rows, rank_part), jnp.float32),
-            pltpu.VMEM((rows, rank_part), jnp.float32),
-            pltpu.VMEM((pairs - 1, rows, rank_part), jnp.float32),
-            dma((3,)),
+            pltpu.VMEM((HALVES, plane - 1, rows, rank_part), jnp.float32),
+            pltpu.VMEM((HALVES, rows, rank_part), jnp.float32),
+            pltpu.VMEM((2 * pairs - 1, rows, rank_part), jnp.float32),
+            dma((5,)),
             dma((2, nz, PIECES)),
             dma((1,)),
             dma((pairs, PIECES)),
@@ -514,17 +571,15 @@
             dma((2, nz)),
             dma((1,)),
             dma((1,)),
-            dma((1,)),
-            dma((1,)),
-            dma((1,)),
-            dma((1,)),
-            dma((1,)),
-            dma((1,)),
+            dma((HALVES,)),
+            dma((HALVES,)),
+            dma((1,)),
+            dma((HALVES,)),
             dma((1,)),
             dma((1,)),
         ],
         compiler_params=pltpu.CompilerParams(
-            collective_id=0, has_side_effects=True, vmem_limit_bytes=40 * 2**20
+            collective_id=0, has_side_effects=True, vmem_limit_bytes=60 * 2**20
         ),
         name="exchange",
     )(slot_column_block, block_live, integral_strips, x_blocks, aux_factor)

time: 125 us -> 112 us (0.90)
  Pallas kernels: 120 us -> 111 us
  local copies, waits for them, and re-layouts: 5.1 us -> 0 us
    pallas_call x1, Pallas kernels: 118 us -> 109 us  [per_device(): pl.pallas_call(exchange_kernel, out_shape=jax.ShapeDtypeStruct((pairs, ro...]
    unnamed x12 -> x0, local copies, waits for them, and re-layouts: 5.1 us -> none
where the time goes in v2:
time: 112 us; the launch traced here: 111 us
  Pallas kernels  111 us (99%)
    pallas_call x1, Pallas kernels, per_device(): pl.pallas_call(exchange_kernel, out_shape=jax.ShapeDtypeStruct((pairs, ro...  109 us

profile of v2, /device:TPU:1, one launch (start us, length us, event | category | flops | bytes accessed | tf_op | source)
XLA Modules:
  0.0 111.4 jit_solution(5352577587267292899)
XLA Ops:
  0.0 109.3 %exchange.1.refs_2_ = f32[16,8,128]{2,1,0:T(8,128)} custom-call(s32[32]{0:T(128)} %cols_hbm.1, s32[32]{0:T(128)} %live_hbm.1, bf16[2,512,640]{2,1,0:T(8,128)(2,1)} %ints_hbm.1, bf16[3,128,128]{2,1,0:T(8,128)(2,1)} %bitcast.2, bf16[256,640]{1,0:T(8,128)(2,1)} %z_hbm.1), custom_call_target="tpu_custom_call" | custom-call | tf_op jit(solution)/shard_map/exchange/pallas_call | solution.py:546
  109.3 2.1 %place.1 = f32[384,128]{1,0:T(8,128)} custom-call(s32[1]{0:T(128)} %bitcast.base, s32[32]{0:T(128)} %refs_0_.1, s32[32]{0:T(128)} %refs_1_.1, f32[16,8,128]{2,1,0:T(8,128)} %exchange.1.refs_2_), custom_call_target="tpu_custom_call" | custom-call | tf_op jit(solution)/shard_map/place/pallas_call | solution.py:588

commit v3 on v2

--- a/solution.py
+++ b/solution.py
@@ -11,10 +11,12 @@
 CORES = 2
 HALVES = 2
 ROW = 4
-PIECES = 2
-LEAD = 3
-EVENTS = {8: (11, 11, 11, 12, 12, 12, 12, 13), 4: (1, 2, 3, 5), 2: (1, 1)}
-PEER_LAG = 6
+PIECES = 4
+X_EVERY = PIECES // 2
+LEAD = 0
+PEER_LAG = 5
+SUM_LAG = 4
+OTHER_LAG = 4
 MESH = pl.DeviceIdType.MESH
 
 
@@ -33,6 +35,7 @@
     xin,
     xout,
     xfull,
+    prod,
     tpart,
     trecv,
     sbuf,
@@ -278,17 +281,21 @@
         some = xfull.at[pl.ds(0, plane - 1)]
         pltpu.make_async_copy(some, some, xg_recv.at[which_half]).wait()
 
-    def contract(shard):
+    def multiply(shard):
         z = zbuf[shard]
         for slot in range(slots):
-            products = lax.dot_general(
+            prod[shard, slot] = lax.dot_general(
                 ibuf[slot], z, (((1,), (1,)), ((), ())), preferred_element_type=jnp.float32
             )
+
+    def contract(shard):
+        for slot in range(slots):
             alive = live_ref[p * slots + slot].astype(jnp.float32)
             for h in range(chunks):
                 chunk = shard * chunks + h
                 rows = xfull[chunk, slot].astype(jnp.float32)
-                part = products[:, h * width : (h + 1) * width].reshape(mus, width, width)
+                part = prod[shard, slot, :, h * width : (h + 1) * width]
+                part = part.reshape(mus, width, width)
                 term = jnp.sum(part * rows[None], axis=1) * alive
                 tpart[chunk, slot * mus : (slot + 1) * mus, :] = term
         for h in range(chunks):
@@ -309,7 +316,7 @@
                     device_id_type=MESH,
                 ).start()
 
-    def contract_set(step):
+    def for_set(step, first, last, what):
         def one(n, _):
             direction = n // CORES
             core = lax.rem(c + n, CORES)
@@ -320,22 +327,30 @@
 
             @pl.when(valid)
             def _():
-                @pl.when(core != c)
-                def _():
-                    for piece in range(PIECES):
-                        z_arrived(shard, piece)
-
-                contract(shard)
+                what(shard, core)
 
             return 0
 
-        lax.fori_loop(0, 2 * CORES, one, 0)
+        lax.fori_loop(first, last, one, 0)
+
+    def multiply_arrived(shard, core):
+        @pl.when(core != c)
+        def _():
+            for piece in range(PIECES):
+                z_arrived(shard, piece)
+
+        multiply(shard)
+
+    def contract_ready(shard, core):
+        contract(shard)
 
     load_z.wait()
     load_i.wait()
 
-    done_at = EVENTS[nz]
     early = nz // 2 - 1
+    ready = PIECES * (nz - 2) + 1
+    done_at = [ready] * early + [min(ready + OTHER_LAG, PIECES * (nz - 1) - 1)] * early
+    done_at += [PIECES * (nz - 1) - 1, PIECES * (nz - 1)]
     own_parity = lax.rem(half + k, 2)
 
     def step_of(item):
@@ -360,8 +375,9 @@
             count = count + (event >= done_at[n]).astype(jnp.int32)
         return count
 
-    last_event = 2 * (nz - 1)
-    x_event = nz - 1 - lead
+    last_event = PIECES * (nz - 1) + 1
+    x_event = X_EVERY * (nz - 1 - lead)
+    shares = 2 * CORES // PIECES
     peer_event = min(x_event + PEER_LAG, done_at[early])
 
     def spread(hh):
@@ -384,8 +400,8 @@
         lax.fori_loop(near, pairs, send, 0)
 
     def event_step(event, _):
-        t = event // 2 + 1
-        piece = lax.rem(event, 2)
+        t = event // PIECES + 1
+        piece = lax.rem(event, PIECES)
 
         @pl.when(k - t >= 0)
         def _():
@@ -407,9 +423,9 @@
 
             z_side_copy(k + t, piece).start()
 
-        @pl.when(event < x_event)
-        def _():
-            x_step(event + lead, 0)
+        @pl.when(jnp.logical_and(event < x_event, lax.rem(event, X_EVERY) == 0))
+        def _():
+            x_step(event // X_EVERY + lead, 0)
 
         @pl.when(event == x_event)
         def _():
@@ -432,12 +448,17 @@
         for hh in range(HALVES):
             step = jnp.abs(k - aux_of(y, hh, x) // (chunks * CORES))
 
-            @pl.when(event == finished_at(item_of(step)) + 1)
+            @pl.when(event == jnp.minimum(finished_at(item_of(step)) + SUM_LAG, last_event))
             def _():
                 spread(hh)
 
+        ending = event == PIECES * (nz - 1)
+        first = jnp.where(ending, 0, piece * shares)
+        last = jnp.where(ending, 2 * CORES, (piece + 1) * shares)
+        for_set(t - 1, first, jnp.where(event > PIECES * (nz - 1), 0, last), multiply_arrived)
+
         def work(item, _):
-            contract_set(step_of(item))
+            for_set(step_of(item), 0, 2 * CORES, contract_ready)
             return 0
 
         lax.fori_loop(items_by(event - 1), items_by(event), work, 0)
@@ -557,6 +578,7 @@
             pltpu.VMEM((2, nz, slots, width, rank_part), jnp.bfloat16),
             pltpu.VMEM((nz, slots, width, rank_part), jnp.bfloat16),
             pltpu.VMEM((auxes, slots, width, rank_part), jnp.bfloat16),
+            pltpu.VMEM((pairs, slots, strip_size, shard_rows), jnp.float32),
             pltpu.VMEM((auxes, rows, rank_part), jnp.float32),
             pltpu.VMEM((HALVES, plane - 1, rows, rank_part), jnp.float32),
             pltpu.VMEM((HALVES, rows, rank_part), jnp.float32),

time: 112 us -> 97.4 us (0.87)
  Pallas kernels: 111 us -> 97.2 us
    pallas_call x1, Pallas kernels: 109 us -> 95.1 us  [per_device(): pl.pallas_call(exchange_kernel, out_shape=jax.ShapeDtypeStruct((pairs, ro...]
where the time goes in v3:
time: 97.4 us; the launch traced here: 97.2 us
  Pallas kernels  97.2 us (100%)
    pallas_call x1, Pallas kernels, per_device(): pl.pallas_call(exchange_kernel, out_shape=jax.ShapeDtypeStruct((pairs, ro...  95.1 us
    pallas_call x1, Pallas kernels, per_device(): pl.pallas_call(lambda base, *refs: place_kernel(base, blocks_dev, width /...  2.11 us

profile of v3, /device:TPU:1, one launch (start us, length us, event | category | flops | bytes accessed | tf_op | source)
XLA Modules:
  0.0 97.2 jit_solution(6288776717728633304)
XLA Ops:
  0.0 95.1 %exchange.1.refs_2_ = f32[16,8,128]{2,1,0:T(8,128)} custom-call(s32[32]{0:T(128)} %cols_hbm.1, s32[32]{0:T(128)} %live_hbm.1, bf16[2,512,640]{2,1,0:T(8,128)(2,1)} %ints_hbm.1, bf16[3,128,128]{2,1,0:T(8,128)(2,1)} %bitcast.2, bf16[256,640]{1,0:T(8,128)(2,1)} %z_hbm.1), custom_call_target="tpu_custom_call" | custom-call | tf_op jit(solution)/shard_map/exchange/pallas_call | solution.py:567
  95.1 2.1 %place.1 = f32[384,128]{1,0:T(8,128)} custom-call(s32[1]{0:T(128)} %bitcast.base, s32[32]{0:T(128)} %refs_0_.1, s32[32]{0:T(128)} %refs_1_.1, f32[16,8,128]{2,1,0:T(8,128)} %exchange.1.refs_2_), custom_call_target="tpu_custom_call" | custom-call | tf_op jit(solution)/shard_map/place/pallas_call | solution.py:610

commit v4 on v3

--- a/solution.py
+++ b/solution.py
@@ -15,8 +15,8 @@
 X_EVERY = PIECES // 2
 LEAD = 0
 PEER_LAG = 5
+WORD_EVENTS = (0, 2, 5, 9)
 SUM_LAG = 4
-OTHER_LAG = 4
 MESH = pl.DeviceIdType.MESH
 
 
@@ -56,6 +56,7 @@
     t1_recv,
     t2_send,
     t2_recv,
+    word_sem,
 ):
     pairs = lax.axis_size("pair")
     auxes = lax.axis_size("aux")
@@ -88,27 +89,35 @@
 
     barrier = pltpu.get_barrier_semaphore()
 
-    def greet_line(rel, _):
-        pl.semaphore_signal(
-            barrier, inc=1, device_id=(lax.rem(p + rel, pairs), j), device_id_type=MESH
-        )
-        return 0
-
-    lax.fori_loop(1, pairs, greet_line, 0)
-
-    def greet_plane(rel, _):
-        pl.semaphore_signal(barrier, inc=1, device_id=(p, plane_aux(rel)), device_id_type=MESH)
-        return 0
-
-    lax.fori_loop(1, plane, greet_plane, 0)
-
-    def greet_peers(rel, _):
-        pl.semaphore_signal(
-            barrier, inc=1, device_id=(lax.rem(p + rel, pairs), peer), device_id_type=MESH
-        )
-        return 0
-
-    lax.fori_loop(0, pairs, greet_peers, 0)
+    def ring(hops):
+        z = lax.rem(half * nz + k + hops + HALVES * nz, HALVES * nz)
+        return lax.rem(z, nz) * CORES + c, aux_of(y, z // nz, x)
+
+    def across(hops):
+        return p, aux_of(y, half, lax.rem(x + hops + ROW, ROW))
+
+    def along(hops):
+        return p, aux_of(lax.rem(y + hops + ny, ny), half, x)
+
+    def greet(semaphore, devices):
+        for device in devices:
+            pl.semaphore_signal(semaphore, inc=1, device_id=device, device_id_type=MESH)
+
+    greet(barrier, [ring(1), ring(-1), (sib, j), across(1), across(-1), along(1), along(-1)])
+
+    word = [
+        [(word_sem.at[0], [across(1), across(-1)]), (word_sem.at[1], [ring(1), ring(-1)])],
+        [(word_sem.at[2], [along(1), along(-1)]), (word_sem.at[3], [ring(2), ring(-2)])],
+        [(word_sem.at[4], [along(1), along(-1)]), (word_sem.at[5], [ring(4), ring(-4)])],
+    ]
+
+    def pass_word(turn):
+        if turn > 0:
+            for semaphore, devices in word[turn - 1]:
+                pl.semaphore_wait(semaphore, len(devices))
+        if turn < len(word):
+            for semaphore, devices in word[turn]:
+                greet(semaphore, devices)
 
     load_i = pltpu.make_async_copy(ints_hbm, ibuf, local_sem.at[0])
     load_z = pltpu.make_async_copy(z_hbm, zbuf.at[p], local_sem.at[1])
@@ -121,7 +130,7 @@
     load_live.start()
     load_z.start()
     load_i.start()
-    pl.semaphore_wait(barrier, 2 * pairs - 1 + plane - 1)
+    pl.semaphore_wait(barrier, 7)
 
     def z_copy(direction, shard_chip, piece, own=False):
         rows = pl.ds(pl.multiple_of(piece * piece_rows, piece_rows), piece_rows)
@@ -320,7 +329,7 @@
         def one(n, _):
             direction = n // CORES
             core = lax.rem(c + n, CORES)
-            chip = jnp.where(direction == 0, k - step, k + step)
+            chip = jnp.where((direction == 0) == (k >= nz // 2), k - step, k + step)
             shard = chip * CORES + core
             valid = jnp.logical_and(chip >= 0, chip < nz)
             valid = jnp.logical_and(valid, jnp.logical_or(step > 0, direction == 0))
@@ -348,9 +357,8 @@
     load_i.wait()
 
     early = nz // 2 - 1
-    ready = PIECES * (nz - 2) + 1
-    done_at = [ready] * early + [min(ready + OTHER_LAG, PIECES * (nz - 1) - 1)] * early
-    done_at += [PIECES * (nz - 1) - 1, PIECES * (nz - 1)]
+    ready = PIECES * (nz - 2)
+    done_at = [ready] * early + [ready + 2] * (early + 1) + [PIECES * (nz - 1)]
     own_parity = lax.rem(half + k, 2)
 
     def step_of(item):
@@ -426,6 +434,12 @@
         @pl.when(jnp.logical_and(event < x_event, lax.rem(event, X_EVERY) == 0))
         def _():
             x_step(event // X_EVERY + lead, 0)
+
+        for turn, at in enumerate(WORD_EVENTS):
+
+            @pl.when(event == min(at, x_event))
+            def _():
+                pass_word(turn)
 
         @pl.when(event == x_event)
         def _():
@@ -599,6 +613,7 @@
             dma((HALVES,)),
             dma((1,)),
             dma((1,)),
+            pltpu.SemaphoreType.REGULAR((6,)),
         ],
         compiler_params=pltpu.CompilerParams(
             collective_id=0, has_side_effects=True, vmem_limit_bytes=60 * 2**20

time: 97.4 us -> 95 us (0.975)
  Pallas kernels: 97.2 us -> 94.8 us
    pallas_call x1, Pallas kernels: 95.1 us -> 92.7 us  [per_device(): pl.pallas_call(exchange_kernel, out_shape=jax.ShapeDtypeStruct((pairs, ro...]
where the time goes in v4:
time: 95 us; the launch traced here: 94.8 us
  Pallas kernels  94.8 us (100%)
    pallas_call x1, Pallas kernels, per_device(): pl.pallas_call(exchange_kernel, out_shape=jax.ShapeDtypeStruct((pairs, ro...  92.7 us
    pallas_call x1, Pallas kernels, per_device(): pl.pallas_call(lambda base, *refs: place_kernel(base, blocks_dev, width /...  2.11 us

profile of v4, /device:TPU:1, one launch (start us, length us, event | category | flops | bytes accessed | tf_op | source)
XLA Modules:
  0.0 94.8 jit_solution(5941854894301616869)
XLA Ops:
  0.0 92.7 %exchange.1.refs_2_ = f32[16,8,128]{2,1,0:T(8,128)} custom-call(s32[32]{0:T(128)} %cols_hbm.1, s32[32]{0:T(128)} %live_hbm.1, bf16[2,512,640]{2,1,0:T(8,128)(2,1)} %ints_hbm.1, bf16[3,128,128]{2,1,0:T(8,128)(2,1)} %bitcast.2, bf16[256,640]{1,0:T(8,128)(2,1)} %z_hbm.1), custom_call_target="tpu_custom_call" | custom-call | tf_op jit(solution)/shard_map/exchange/pallas_call | solution.py:581
  92.7 2.1 %place.1 = f32[384,128]{1,0:T(8,128)} custom-call(s32[1]{0:T(128)} %bitcast.base, s32[32]{0:T(128)} %refs_0_.1, s32[32]{0:T(128)} %refs_1_.1, f32[16,8,128]{2,1,0:T(8,128)} %exchange.1.refs_2_), custom_call_target="tpu_custom_call" | custom-call | tf_op jit(solution)/shard_map/place/pallas_call | solution.py:625

commit v5 on v4

--- a/solution.py
+++ b/solution.py
@@ -15,6 +15,7 @@
 X_EVERY = PIECES // 2
 LEAD = 0
 PEER_LAG = 5
+ON_LAG = 3
 WORD_EVENTS = (0, 2, 5, 9)
 SUM_LAG = 4
 MESH = pl.DeviceIdType.MESH
@@ -244,7 +245,7 @@
 
     x_peer = pltpu.make_async_remote_copy(
         src_ref=xout.at[k],
-        dst_ref=xfull.at[j],
+        dst_ref=xfull.at[y, half, x],
         send_sem=xpeer_send.at[0],
         recv_sem=xpeer_recv.at[0],
         device_id=(p, peer),
@@ -269,26 +270,42 @@
                 total = xout[k, slot].astype(jnp.float32) + xin[1, k, slot].astype(jnp.float32)
                 xout[k, slot] = total.astype(xout.dtype)
 
-        xfull[j] = xout[k]
+        xfull[y, half, x] = xout[k]
         x_peer.start()
 
-    def x_plane(which, which_half):
-        def body(rel, _):
+    def gathered(hh, kind):
+        if kind == 0:
+            return xfull.at[y, hh, x, 0], xfull.at[0, hh, pl.ds(0, ROW - 1), 0], across, ROW
+        if kind == 1:
+            return xfull.at[y, hh, x, 1], xfull.at[pl.ds(0, ny - 1), hh, 0, 1], along, ny
+        if kind == 2:
+            return xfull.at[y, hh, :, 0], xfull.at[pl.ds(0, ny - 1), hh, :, 0], along, ny
+        return xfull.at[:, hh, x, 1], xfull.at[:, hh, pl.ds(0, ROW - 1), 1], across, ROW
+
+    def x_gather(hh, stage, kind):
+        block, _, line, length = gathered(hh, kind)
+        for hops in range(1, length):
             pltpu.make_async_remote_copy(
-                src_ref=xfull.at[which],
-                dst_ref=xfull.at[which],
-                send_sem=xg_send.at[which_half],
-                recv_sem=xg_recv.at[which_half],
-                device_id=(p, plane_aux(rel)),
+                src_ref=block,
+                dst_ref=block,
+                send_sem=xg_send.at[stage, kind],
+                recv_sem=xg_recv.at[stage, kind],
+                device_id=line(hops),
                 device_id_type=MESH,
             ).start()
-            return 0
-
-        lax.fori_loop(1, plane, body, 0)
-
-    def x_plane_arrived(which_half):
-        some = xfull.at[pl.ds(0, plane - 1)]
-        pltpu.make_async_copy(some, some, xg_recv.at[which_half]).wait()
+
+    def x_gathered(stage, kind, semaphore):
+        _, some, _, _ = gathered(0, kind)
+        pltpu.make_async_copy(some, some, semaphore.at[stage, kind]).wait()
+
+    def x_gather_on(hh, stage):
+        for kind in range(2):
+            x_gathered(stage, kind, xg_recv)
+            x_gather(hh, stage, kind + 2)
+
+    def x_plane_arrived(stage):
+        for kind in range(2, 4):
+            x_gathered(stage, kind, xg_recv)
 
     def multiply(shard):
         z = zbuf[shard]
@@ -302,7 +319,8 @@
             alive = live_ref[p * slots + slot].astype(jnp.float32)
             for h in range(chunks):
                 chunk = shard * chunks + h
-                rows = xfull[chunk, slot].astype(jnp.float32)
+                yy, hh, xx = chunk // (HALVES * ROW), (chunk // ROW) % HALVES, chunk % ROW
+                rows = xfull[yy, hh, xx, slot].astype(jnp.float32)
                 part = prod[shard, slot, :, h * width : (h + 1) * width]
                 part = part.reshape(mus, width, width)
                 term = jnp.sum(part * rows[None], axis=1) * alive
@@ -444,12 +462,22 @@
         @pl.when(event == x_event)
         def _():
             x_last()
-            x_plane(j, 0)
+            x_gather(half, 0, 0)
+            x_gather(half, 0, 1)
 
         @pl.when(event == peer_event)
         def _():
-            pltpu.make_async_copy(xfull.at[0], xfull.at[0], xpeer_recv.at[0]).wait()
-            x_plane(peer, 1)
+            pltpu.make_async_copy(xout.at[0], xout.at[0], xpeer_recv.at[0]).wait()
+            x_gather(1 - half, 1, 0)
+            x_gather(1 - half, 1, 1)
+
+        @pl.when(event == min(x_event + ON_LAG, done_at[0]))
+        def _():
+            x_gather_on(half, 0)
+
+        @pl.when(event == min(peer_event + ON_LAG, done_at[early]))
+        def _():
+            x_gather_on(1 - half, 1)
 
         @pl.when(event == done_at[0])
         def _():
@@ -481,6 +509,38 @@
 
     lax.fori_loop(0, last_event + 1, event_step, 0)
 
+    x_side.wait_send()
+    x_peer.wait_send()
+    pltpu.make_async_copy(trecv, trecv, t1_send.at[0]).wait()
+    for stage in range(HALVES):
+        for kind in range(4):
+            x_gathered(stage, kind, xg_send)
+    sent_z = zbuf.at[pl.ds(0, nz)]
+    pltpu.make_async_copy(sent_z, sent_z, z_side.at[0]).wait()
+
+    def z_sent(chip, _):
+        @pl.when(jnp.logical_and(chip <= k, k < nz - 1))
+        def _():
+            for piece in range(PIECES):
+                z_copy(0, chip, piece).wait_send()
+
+        @pl.when(jnp.logical_and(chip >= k, k > 0))
+        def _():
+            for piece in range(PIECES):
+                z_copy(1, chip, piece).wait_send()
+
+        @pl.when(chip > k)
+        def _():
+            x_copy(0, chip).wait_send()
+
+        @pl.when(chip < k)
+        def _():
+            x_copy(1, chip).wait_send()
+
+        return 0
+
+    lax.fori_loop(0, nz, z_sent, 0)
+
     pltpu.make_async_copy(fin, fin, t2_recv.at[0]).wait()
     out_ref[p] = sbuf[half] + fin[pairs - 1]
 
@@ -489,39 +549,7 @@
         return 0
 
     lax.fori_loop(1, pairs, take, 0)
-
-    x_side.wait_send()
-    x_peer.wait_send()
     pltpu.make_async_copy(fin, fin, t2_send.at[0]).wait()
-    pltpu.make_async_copy(trecv, trecv, t1_send.at[0]).wait()
-    sent = xfull.at[pl.ds(0, plane - 1)]
-    for which in range(HALVES):
-        pltpu.make_async_copy(sent, sent, xg_send.at[which]).wait()
-    sent_z = zbuf.at[pl.ds(0, nz)]
-    pltpu.make_async_copy(sent_z, sent_z, z_side.at[0]).wait()
-
-    def z_sent(chip, _):
-        @pl.when(jnp.logical_and(chip <= k, k < nz - 1))
-        def _():
-            for piece in range(PIECES):
-                z_copy(0, chip, piece).wait_send()
-
-        @pl.when(jnp.logical_and(chip >= k, k > 0))
-        def _():
-            for piece in range(PIECES):
-                z_copy(1, chip, piece).wait_send()
-
-        @pl.when(chip > k)
-        def _():
-            x_copy(0, chip).wait_send()
-
-        @pl.when(chip < k)
-        def _():
-            x_copy(1, chip).wait_send()
-
-        return 0
-
-    lax.fori_loop(0, nz, z_sent, 0)
 
 
 def place_kernel(first_block, blocks_dev, strips, slots, rows_ref, strip_ref, sums_ref, out_ref):
@@ -591,7 +619,7 @@
             pltpu.VMEM((CORES * blocks_dev, width, rank_part), jnp.bfloat16),
             pltpu.VMEM((2, nz, slots, width, rank_part), jnp.bfloat16),
             pltpu.VMEM((nz, slots, width, rank_part), jnp.bfloat16),
-            pltpu.VMEM((auxes, slots, width, rank_part), jnp.bfloat16),
+            pltpu.VMEM((plane // ROW, HALVES, ROW, slots, width, rank_part), jnp.bfloat16),
             pltpu.VMEM((pairs, slots, strip_size, shard_rows), jnp.float32),
             pltpu.VMEM((auxes, rows, rank_part), jnp.float32),
             pltpu.VMEM((HALVES, plane - 1, rows, rank_part), jnp.float32),
@@ -607,8 +635,8 @@
             dma((2, nz)),
             dma((1,)),
             dma((1,)),
-            dma((HALVES,)),
-            dma((HALVES,)),
+            dma((HALVES, 4)),
+            dma((HALVES, 4)),
             dma((1,)),
             dma((HALVES,)),
             dma((1,)),

time: 95 us -> 92 us (0.968)
  Pallas kernels: 94.8 us -> 91.8 us
    pallas_call x1, Pallas kernels: 92.7 us -> 89.7 us  [per_device(): pl.pallas_call(exchange_kernel, out_shape=jax.ShapeDtypeStruct((pairs, ro...]
where the time goes in v5:
time: 92 us; the launch traced here: 91.8 us
  Pallas kernels  91.8 us (100%)
    pallas_call x1, Pallas kernels, per_device(): pl.pallas_call(exchange_kernel, out_shape=jax.ShapeDtypeStruct((pairs, ro...  89.7 us
    pallas_call x1, Pallas kernels, per_device(): pl.pallas_call(lambda base, *refs: place_kernel(base, blocks_dev, width /...  2.11 us

profile of v5, /device:TPU:1, one launch (start us, length us, event | category | flops | bytes accessed | tf_op | source)
XLA Modules:
  0.0 91.8 jit_solution(9783401101132532770)
XLA Ops:
  0.0 89.7 %exchange.1.refs_2_ = f32[16,8,128]{2,1,0:T(8,128)} custom-call(s32[32]{0:T(128)} %cols_hbm.1, s32[32]{0:T(128)} %live_hbm.1, bf16[2,512,640]{2,1,0:T(8,128)(2,1)} %ints_hbm.1, bf16[3,128,128]{2,1,0:T(8,128)(2,1)} %bitcast.2, bf16[256,640]{1,0:T(8,128)(2,1)} %z_hbm.1), custom_call_target="tpu_custom_call" | custom-call | tf_op jit(solution)/shard_map/exchange/pallas_call | solution.py:609
  89.7 2.1 %place.1 = f32[384,128]{1,0:T(8,128)} custom-call(s32[1]{0:T(128)} %bitcast.base, s32[32]{0:T(128)} %refs_0_.1, s32[32]{0:T(128)} %refs_1_.1, f32[16,8,128]{2,1,0:T(8,128)} %exchange.1.refs_2_), custom_call_target="tpu_custom_call" | custom-call | tf_op jit(solution)/shard_map/place/pallas_call | solution.py:653

commit v6 on v5

--- a/solution.py
+++ b/solution.py
@@ -487,7 +487,7 @@
         def _():
             x_plane_arrived(1)
 
-        for hh in range(HALVES):
+        for hh in (1 - half, half):
             step = jnp.abs(k - aux_of(y, hh, x) // (chunks * CORES))
 
             @pl.when(event == jnp.minimum(finished_at(item_of(step)) + SUM_LAG, last_event))

time: 92 us -> 92 us (level)
  no operation moved by 1% of the time
where the time goes in v6:
time: 92 us; the launch traced here: 91.8 us
  Pallas kernels  91.8 us (100%)
    pallas_call x1, Pallas kernels, per_device(): pl.pallas_call(exchange_kernel, out_shape=jax.ShapeDtypeStruct((pairs, ro...  89.7 us
    pallas_call x1, Pallas kernels, per_device(): pl.pallas_call(lambda base, *refs: place_kernel(base, blocks_dev, width /...  2.1 us

profile of v6, /device:TPU:1, one launch (start us, length us, event | category | flops | bytes accessed | tf_op | source)
XLA Modules:
  0.0 91.8 jit_solution(11612954425551142955)
XLA Ops:
  0.0 89.7 %exchange.1.refs_2_ = f32[16,8,128]{2,1,0:T(8,128)} custom-call(s32[32]{0:T(128)} %cols_hbm.1, s32[32]{0:T(128)} %live_hbm.1, bf16[2,512,640]{2,1,0:T(8,128)(2,1)} %ints_hbm.1, bf16[3,128,128]{2,1,0:T(8,128)(2,1)} %bitcast.2, bf16[256,640]{1,0:T(8,128)(2,1)} %z_hbm.1), custom_call_target="tpu_custom_call" | custom-call | tf_op jit(solution)/shard_map/exchange/pallas_call | solution.py:609
  89.7 2.1 %place.1 = f32[384,128]{1,0:T(8,128)} custom-call(s32[1]{0:T(128)} %bitcast.base, s32[32]{0:T(128)} %refs_0_.1, s32[32]{0:T(128)} %refs_1_.1, f32[16,8,128]{2,1,0:T(8,128)} %exchange.1.refs_2_), custom_call_target="tpu_custom_call" | custom-call | tf_op jit(solution)/shard_map/place/pallas_call | solution.py:653
